TPU v7x, 512 devices: a whole 4x4x16 slice. The times are simulated.
512 devices in a mesh: gx: 64 (over z, x_lo, core), gy: 8 (over y, x_hi).
Axes of the slice: x: 4 (x_hi: 2, x_lo: 2; x = x_hi * 2 + x_lo), y: 4, z: 16, core: 2. Of those that a mesh axis runs over, the one named last changes fastest.
Arguments:
- grad_late: float32 [2, 20, 512, 1024], P(None, None, 'gx', 'gy'), may hold values from -6 to 6
- grad_early: float32 [2, 20, 512, 1024], P(None, None, 'gx', 'gy'), may hold values from -6 to 6
- accumulation: bfloat16 [4, 20, 512, 1024], P(None, None, 'gx', 'gy'), may hold values from -0.021 to 0.302, as said below
- mobility_late: bfloat16 [4, 20, 512, 1024], P(None, None, 'gx', 'gy'), may hold values from -0.25 to 1.4, as said below
- mobility_early: bfloat16 [4, 20, 512, 1024], P(None, None, 'gx', 'gy'), may hold values from -0.25 to 1.4, as said below
- trans_x: bfloat16 [20, 512, 1024], P(None, 'gx', 'gy'), may hold values from 0.0099487305 to 1
- trans_y: bfloat16 [20, 512, 1024], P(None, 'gx', 'gy'), may hold values from 0.0099487305 to 1
- trans_z: bfloat16 [20, 512, 1024], P(None, 'gx', 'gy'), may hold values from 0.0099487305 to 1
- perf_cell: int32 [64, 8, 256], P('gx', 'gy'), may hold values from 0 to 20479
- perf_well: int32 [64, 8, 256], P('gx', 'gy'), may hold values from 0 to 511
- productivity: float32 [64, 8, 256], P('gx', 'gy'), may hold values from 0.3 to 3
Outputs:
- adjoint_early: float32 [2, 20, 512, 1024], P(None, None, 'gx', 'gy')
- well_partials: float32 [4, 512], P(None, 'gx')
Inputs may be any that keep to these rules, and one draw needn't show every extreme that they name: `accumulation`: off-diagonal entries c1, c2 lie within 0.021 in magnitude, diagonal entries c0, c3 from 0.05 to 0.302. `mobility_late`: off-diagonal entries b1, b2 lie within 0.25 in magnitude, diagonal entries b0, b3 from 0.6 to 1.4. `mobility_early`: off-diagonal entries b1, b2 lie within 0.25 in magnitude, diagonal entries b0, b3 from 0.6 to 1.4.
All inputs are finite; a program needn't handle non-finite values.
Results may differ from a plain program's by a relative error of at most 0.0003.
Values may be sent and summed in bfloat16 or wider, within the bound.
A program may use at most 64 MiB of HBM per device.

v0:
```python
import jax
import jax.numpy as jnp
from jax import lax
from jax.sharding import PartitionSpec as P

SWEEPS = 3
WELL_DEV = 8


def shifted(block, axis, distance):
    devices = range(lax.axis_size(axis))
    route = [(i - distance, i) for i in devices if i - distance in devices]
    return lax.ppermute(block, axis, route)


def extended(cells, sides, width):
    for axis, dim in sides:
        count = lax.axis_size(axis)
        ends = count - 1
        head = lax.slice_in_dim(cells, 0, width, axis=dim)
        tail = lax.slice_in_dim(cells, cells.shape[dim] - width, cells.shape[dim], axis=dim)
        cells = jnp.concatenate(
            [
                lax.ppermute(tail, axis, [(i, (i + 1) % count) for i in range(ends)]),
                cells,
                lax.ppermute(head, axis, [((i + 1) % count, i) for i in range(ends)]),
            ],
            axis=dim,
        )
    return cells


def transpose_apply(matrix, vector):
    return jnp.stack(
        [
            matrix[0] * vector[0] + matrix[2] * vector[1],
            matrix[1] * vector[0] + matrix[3] * vector[1],
        ]
    )


def face_total(padded_x, padded_y, layer_trans):
    upper_trans = jnp.concatenate([layer_trans[1:], jnp.zeros_like(layer_trans[:1])], 0)
    return (
        padded_x[:, 1:-1, 1:-1]
        + padded_x[:, 2:, 1:-1]
        + padded_y[:, 1:-1, 1:-1]
        + padded_y[:, 1:-1, 2:]
        + layer_trans
        + upper_trans
    )


def diag_inverse(padded_x, padded_y, layer_trans, accum_full, mobility, inside):
    facesum = face_total(padded_x, padded_y, layer_trans)
    diag_block = accum_full + facesum[None] * mobility
    determinant = diag_block[0] * diag_block[3] - diag_block[1] * diag_block[2]
    determinant = jnp.where(inside > 0, determinant, jnp.float32(1.0))
    det_scale = inside / determinant
    return jnp.stack(
        [
            diag_block[3] * det_scale,
            -diag_block[1] * det_scale,
            -diag_block[2] * det_scale,
            diag_block[0] * det_scale,
        ]
    )


def jacobi_sweep(adjoint_pad, padded_x, padded_y, layer_trans, source, mobility, inverse):
    centre = adjoint_pad[:, :, 1:-1, 1:-1]
    inflow = (
        padded_x[None, :, 1:-1, 1:-1] * adjoint_pad[:, :, :-2, 1:-1]
        + padded_x[None, :, 2:, 1:-1] * adjoint_pad[:, :, 2:, 1:-1]
    )
    inflow = (
        inflow
        + padded_y[None, :, 1:-1, 1:-1] * adjoint_pad[:, :, 1:-1, :-2]
        + padded_y[None, :, 1:-1, 2:] * adjoint_pad[:, :, 1:-1, 2:]
    )
    zero_layer = jnp.zeros_like(centre[:, :1])
    lower_cell = jnp.concatenate([zero_layer, centre[:, :-1]], 1)
    upper_cell = jnp.concatenate([centre[:, 1:], zero_layer], 1)
    upper_trans = jnp.concatenate([layer_trans[1:], jnp.zeros_like(layer_trans[:1])], 0)
    inflow = inflow + layer_trans[None] * lower_cell + upper_trans[None] * upper_cell
    return transpose_apply(inverse, source + transpose_apply(mobility, inflow))


def per_device(
    grad_late,
    grad_early,
    accumulation,
    mobility_late,
    mobility_early,
    trans_x,
    trans_y,
    trans_z,
    perf_cell,
    perf_well,
    productivity,
):
    layers, rows, columns = trans_x.shape
    row_ids = lax.axis_index("gx") * rows + jnp.arange(rows)
    col_ids = lax.axis_index("gy") * columns + jnp.arange(columns)
    layer_ids = jnp.arange(layers)
    masked_x = trans_x.astype(jnp.float32) * (row_ids > 0).astype(jnp.float32)[None, :, None]
    masked_y = trans_y.astype(jnp.float32) * (col_ids > 0).astype(jnp.float32)[None, None, :]
    masked_z = trans_z.astype(jnp.float32) * (layer_ids > 0).astype(jnp.float32)[:, None, None]
    above_x = shifted(masked_x[:, :1, :].astype(jnp.bfloat16), "gx", -1).astype(jnp.float32)
    above_y = shifted(masked_y[:, :, :1].astype(jnp.bfloat16), "gy", -1).astype(jnp.float32)
    padded_x = jnp.concatenate([jnp.zeros_like(above_x), masked_x, above_x], 1)
    padded_x = jnp.pad(padded_x, ((0, 0), (0, 0), (1, 1)))
    padded_y = jnp.concatenate([jnp.zeros_like(above_y), masked_y, above_y], 2)
    padded_y = jnp.pad(padded_y, ((0, 0), (1, 1), (0, 0)))
    inside = jnp.ones((layers, rows, columns), jnp.float32)
    accum_full = accumulation.astype(jnp.float32)

    def solve(source, mobility_arg):
        mobility = mobility_arg.astype(jnp.float32)
        inverse = diag_inverse(padded_x, padded_y, masked_z, accum_full, mobility, inside)
        adjoint = transpose_apply(inverse, source)
        for sweep_index in range(SWEEPS):
            adjoint_pad = extended(adjoint, (("gx", 2), ("gy", 3)), 1)
            adjoint = jacobi_sweep(
                adjoint_pad, padded_x, padded_y, masked_z, source, mobility, inverse
            )
        return adjoint

    adjoint_late = solve(grad_late, mobility_late)
    adjoint_early = solve(grad_early + transpose_apply(accum_full, adjoint_late), mobility_early)
    values = jnp.concatenate([adjoint_early, adjoint_late], 0).reshape(4, -1)
    cell_ids = perf_cell.reshape(-1)
    well_ids = perf_well.reshape(-1)
    picked = jnp.take(values, cell_ids, axis=1) * productivity.reshape(-1)[None]
    nwells = WELL_DEV * lax.axis_size("gx")
    onehot = (well_ids[:, None] == jnp.arange(nwells)[None, :]).astype(jnp.float32)
    partial_value = jnp.dot(
        picked, onehot, precision=lax.Precision.HIGHEST, preferred_element_type=jnp.float32
    )
    owned = lax.psum_scatter(partial_value, "gx", scatter_dimension=1, tiled=True)
    well_partials = lax.psum(owned, "gy")
    return (adjoint_early, well_partials)


def solution(mesh):
    return jax.shard_map(
        per_device,
        mesh=mesh,
        in_specs=(
            P(None, None, "gx", "gy"),
            P(None, None, "gx", "gy"),
            P(None, None, "gx", "gy"),
            P(None, None, "gx", "gy"),
            P(None, None, "gx", "gy"),
            P(None, "gx", "gy"),
            P(None, "gx", "gy"),
            P(None, "gx", "gy"),
            P("gx", "gy", None),
            P("gx", "gy", None),
            P("gx", "gy", None),
        ),
        out_specs=(P(None, None, "gx", "gy"), P(None, "gx")),
        check_vma=False,
    )
```

profile of v0, /device:TPU:128, one launch (start us, length us, event | category | flops | bytes accessed | tf_op | source)
XLA Modules:
  0.0 320.5 jit_solution(5821516998994916361)
XLA Ops:
  15.2 5.9 %collective-permute-start.3 = (f32[2,20,1,128]{3,2,1,0:T(1,128)S(1)}, f32[2,20,1,128]{3,2,1,0:T(1,128)S(1)}, u32[]{:S(2)}, u32[]{:S(2)}) collective-permute-start(f32[2,20,1,128]{3,2,1,0:T(1,128)S(1)} %get-tuple-element.68), channel_id=1, source_target_pairs={{8,0},{16,8},{24,16},{32,24},{40,32},{48,40},{56,48},{64,56},{72,6... | collective-permute-start | bytes 61448 | tf_op jit(solution)/shard_map/ppermute | solution.py:26
  22.7 5.8 %collective-permute-start.4 = (f32[2,20,10,1]{3,2,1,0:T(8,128)S(1)}, f32[2,20,10,1]{3,2,1,0:T(8,128)S(1)}, u32[]{:S(2)}, u32[]{:S(2)}) collective-permute-start(f32[2,20,10,1]{3,2,1,0:T(8,128)S(1)} %get-tuple-element.43), channel_id=1, source_target_pairs={{0,1},{1,2},{2,3},{3,4},{4,5},{5,6},{6,7},{8,9},{9,10},{10,11},{11... | collective-permute-start | bytes 4808 | tf_op jit(solution)/shard_map/ppermute | solution.py:24
  29.9 5.0 %collective-permute-done.4 = f32[2,20,10,1]{3,2,1,0:T(8,128)S(1)} collective-permute-done((f32[2,20,10,1]{3,2,1,0:T(8,128)S(1)}, f32[2,20,10,1]{3,2,1,0:T(8,128)S(1)}, u32[]{:S(2)}, u32[]{:S(2)}) %collective-permute-start.4) | collective-permute-done | bytes 1632 | tf_op jit(solution)/shard_map/ppermute | solution.py:24
  34.9 9.3 %collective-permute-done.5 = f32[2,20,10,1]{3,2,1,0:T(8,128)S(1)} collective-permute-done((f32[2,20,10,1]{3,2,1,0:T(8,128)S(1)}, f32[2,20,10,1]{3,2,1,0:T(8,128)S(1)}, u32[]{:S(2)}, u32[]{:S(2)}) %collective-permute-start.5) | collective-permute-done | bytes 1632 | tf_op jit(solution)/shard_map/ppermute | solution.py:26
  47.5 5.8 %collective-permute-start.7 = (f32[2,20,1,128]{3,2,1,0:T(1,128)S(1)}, f32[2,20,1,128]{3,2,1,0:T(1,128)S(1)}, u32[]{:S(2)}, u32[]{:S(2)}) collective-permute-start(f32[2,20,1,128]{3,2,1,0:T(1,128)S(1)} %get-tuple-element.64), channel_id=1, source_target_pairs={{8,0},{16,8},{24,16},{32,24},{40,32},{48,40},{56,48},{64,56},{72,6... | collective-permute-start | bytes 61448 | tf_op jit(solution)/shard_map/ppermute | solution.py:26
  54.9 4.6 %collective-permute-start.8 = (f32[2,20,10,1]{3,2,1,0:T(8,128)S(1)}, f32[2,20,10,1]{3,2,1,0:T(8,128)S(1)}, u32[]{:S(2)}, u32[]{:S(2)}) collective-permute-start(f32[2,20,10,1]{3,2,1,0:T(8,128)S(1)} %get-tuple-element.41), channel_id=1, source_target_pairs={{0,1},{1,2},{2,3},{3,4},{4,5},{5,6},{6,7},{8,9},{9,10},{10,11},{11... | collective-permute-start | bytes 4808 | tf_op jit(solution)/shard_map/ppermute | solution.py:24
  64.1 9.3 %collective-permute-done.9 = f32[2,20,10,1]{3,2,1,0:T(8,128)S(1)} collective-permute-done((f32[2,20,10,1]{3,2,1,0:T(8,128)S(1)}, f32[2,20,10,1]{3,2,1,0:T(8,128)S(1)}, u32[]{:S(2)}, u32[]{:S(2)}) %collective-permute-start.9) | collective-permute-done | bytes 1632 | tf_op jit(solution)/shard_map/ppermute | solution.py:26
  75.8 5.8 %collective-permute-start.11 = (f32[2,20,1,128]{3,2,1,0:T(1,128)S(1)}, f32[2,20,1,128]{3,2,1,0:T(1,128)S(1)}, u32[]{:S(2)}, u32[]{:S(2)}) collective-permute-start(f32[2,20,1,128]{3,2,1,0:T(1,128)S(1)} %get-tuple-element.60), channel_id=1, source_target_pairs={{8,0},{16,8},{24,16},{32,24},{40,32},{48,40},{56,48},{64,56},{72,6... | collective-permute-start | bytes 61448 | tf_op jit(solution)/shard_map/ppermute | solution.py:26
  83.2 4.5 %collective-permute-start.12 = (f32[2,20,10,1]{3,2,1,0:T(8,128)S(1)}, f32[2,20,10,1]{3,2,1,0:T(8,128)S(1)}, u32[]{:S(2)}, u32[]{:S(2)}) collective-permute-start(f32[2,20,10,1]{3,2,1,0:T(8,128)S(1)} %get-tuple-element.39), channel_id=1, source_target_pairs={{0,1},{1,2},{2,3},{3,4},{4,5},{5,6},{6,7},{8,9},{9,10},{10,11},{11... | collective-permute-start | bytes 4808 | tf_op jit(solution)/shard_map/ppermute | solution.py:24
  89.0 4.4 %collective-permute-done.12 = f32[2,20,10,1]{3,2,1,0:T(8,128)S(1)} collective-permute-done((f32[2,20,10,1]{3,2,1,0:T(8,128)S(1)}, f32[2,20,10,1]{3,2,1,0:T(8,128)S(1)}, u32[]{:S(2)}, u32[]{:S(2)}) %collective-permute-start.12) | collective-permute-done | bytes 1632 | tf_op jit(solution)/shard_map/ppermute | solution.py:24
  93.4 9.3 %collective-permute-done.13 = f32[2,20,10,1]{3,2,1,0:T(8,128)S(1)} collective-permute-done((f32[2,20,10,1]{3,2,1,0:T(8,128)S(1)}, f32[2,20,10,1]{3,2,1,0:T(8,128)S(1)}, u32[]{:S(2)}, u32[]{:S(2)}) %collective-permute-start.13) | collective-permute-done | bytes 1632 | tf_op jit(solution)/shard_map/ppermute | solution.py:26
  105.3 5.8 %collective-permute-start.15 = (f32[2,20,1,128]{3,2,1,0:T(1,128)S(1)}, f32[2,20,1,128]{3,2,1,0:T(1,128)S(1)}, u32[]{:S(2)}, u32[]{:S(2)}) collective-permute-start(f32[2,20,1,128]{3,2,1,0:T(1,128)S(1)} %get-tuple-element.58), channel_id=1, source_target_pairs={{8,0},{16,8},{24,16},{32,24},{40,32},{48,40},{56,48},{64,56},{72,6... | collective-permute-start | bytes 61448 | tf_op jit(solution)/shard_map/ppermute | solution.py:26
  117.9 4.0 %collective-permute-done.16 = f32[2,20,10,1]{3,2,1,0:T(8,128)S(1)} collective-permute-done((f32[2,20,10,1]{3,2,1,0:T(8,128)S(1)}, f32[2,20,10,1]{3,2,1,0:T(8,128)S(1)}, u32[]{:S(2)}, u32[]{:S(2)}) %collective-permute-start.16) | collective-permute-done | bytes 1632 | tf_op jit(solution)/shard_map/ppermute | solution.py:24
  121.9 7.8 %collective-permute-done.17 = f32[2,20,10,1]{3,2,1,0:T(8,128)S(1)} collective-permute-done((f32[2,20,10,1]{3,2,1,0:T(8,128)S(1)}, f32[2,20,10,1]{3,2,1,0:T(8,128)S(1)}, u32[]{:S(2)}, u32[]{:S(2)}) %collective-permute-start.17) | collective-permute-done | bytes 1632 | tf_op jit(solution)/shard_map/ppermute | solution.py:26
  132.0 5.8 %collective-permute-start.19 = (f32[2,20,1,128]{3,2,1,0:T(1,128)S(1)}, f32[2,20,1,128]{3,2,1,0:T(1,128)S(1)}, u32[]{:S(2)}, u32[]{:S(2)}) collective-permute-start(f32[2,20,1,128]{3,2,1,0:T(1,128)S(1)} %get-tuple-element.54), channel_id=1, source_target_pairs={{8,0},{16,8},{24,16},{32,24},{40,32},{48,40},{56,48},{64,56},{72,6... | collective-permute-start | bytes 61448 | tf_op jit(solution)/shard_map/ppermute | solution.py:26
  142.7 4.5 %collective-permute-done.20 = f32[2,20,10,1]{3,2,1,0:T(8,128)S(1)} collective-permute-done((f32[2,20,10,1]{3,2,1,0:T(8,128)S(1)}, f32[2,20,10,1]{3,2,1,0:T(8,128)S(1)}, u32[]{:S(2)}, u32[]{:S(2)}) %collective-permute-start.20) | collective-permute-done | bytes 1632 | tf_op jit(solution)/shard_map/ppermute | solution.py:24
  147.2 7.8 %collective-permute-done.21 = f32[2,20,10,1]{3,2,1,0:T(8,128)S(1)} collective-permute-done((f32[2,20,10,1]{3,2,1,0:T(8,128)S(1)}, f32[2,20,10,1]{3,2,1,0:T(8,128)S(1)}, u32[]{:S(2)}, u32[]{:S(2)}) %collective-permute-start.21) | collective-permute-done | bytes 1632 | tf_op jit(solution)/shard_map/ppermute | solution.py:26
  157.3 5.8 %collective-permute-start.23 = (f32[2,20,1,128]{3,2,1,0:T(1,128)S(1)}, f32[2,20,1,128]{3,2,1,0:T(1,128)S(1)}, u32[]{:S(2)}, u32[]{:S(2)}) collective-permute-start(f32[2,20,1,128]{3,2,1,0:T(1,128)S(1)} %get-tuple-element.50), channel_id=1, source_target_pairs={{8,0},{16,8},{24,16},{32,24},{40,32},{48,40},{56,48},{64,56},{72,6... | collective-permute-start | bytes 61448 | tf_op jit(solution)/shard_map/ppermute | solution.py:26
  168.1 3.9 %collective-permute-done.24 = f32[2,20,10,1]{3,2,1,0:T(8,128)S(1)} collective-permute-done((f32[2,20,10,1]{3,2,1,0:T(8,128)S(1)}, f32[2,20,10,1]{3,2,1,0:T(8,128)S(1)}, u32[]{:S(2)}, u32[]{:S(2)}) %collective-permute-start.24) | collective-permute-done | bytes 1632 | tf_op jit(solution)/shard_map/ppermute | solution.py:24
  172.0 7.8 %collective-permute-done.25 = f32[2,20,10,1]{3,2,1,0:T(8,128)S(1)} collective-permute-done((f32[2,20,10,1]{3,2,1,0:T(8,128)S(1)}, f32[2,20,10,1]{3,2,1,0:T(8,128)S(1)}, u32[]{:S(2)}, u32[]{:S(2)}) %collective-permute-start.25) | collective-permute-done | bytes 1632 | tf_op jit(solution)/shard_map/ppermute | solution.py:26
  181.1 5.5 %copy.17 = f32[4,20480]{0,1:T(8,128)} copy(f32[4,20480]{1,0:T(4,128)S(1)} %pad_maximum_fusion.6) | data formatting | bytes 655360 | tf_op jit(solution)/shard_map/concatenate | solution.py:131
  186.7 4.7 %gather_fusion = f32[256,4]{1,0:T(8,128)S(1)} fusion(f32[4,20480]{0,1:T(8,128)} %copy.17, s32[1024]{0:T(1024)S(1)} %pad_clamp_fusion), kind=kCustom, calls=%fused_computation | custom fusion | bytes 9216 | tf_op jit(solution)/shard_map/jit(_take)/gather | solution.py:134
  191.8 108.2 %all-reduce.13 = f32[4,512]{1,0:T(4,128)S(1)} all-reduce(f32[4,512]{1,0:T(4,128)S(1)} %fusion), channel_id=2, replica_groups=mesh['gx'=64,'gy'=8] {'gx'}, use_global_device_ids=true, to_apply=%region_0.1.clone | all-reduce | flops 2048 | bytes 16384
  300.0 20.5 %psum.7 = f32[4,8]{1,0:T(4,128)} all-reduce(f32[4,8]{1,0:T(4,128)S(1)} %constant_dynamic-slice_fusion), channel_id=1, replica_groups=mesh['gx'=64,'gy'=8] {'gy'}, use_global_device_ids=true, to_apply=%region_1.2 | all-reduce | flops 32 | bytes 256 | tf_op jit(solution)/shard_map/psum | solution.py:141
  (123 shorter events, 57.0 us)
Async XLA Ops:
  1.6 7.4 %collective-permute-start.1 = (bf16[20,8,1]{2,1,0:T(8,128)(2,1)S(1)}, bf16[20,8,1]{2,1,0:T(8,128)(2,1)S(1)}, u32[]{:S(2)}, u32[]{:S(2)}) collective-permute-start(bf16[20,8,1]{2,1,0:T(8,128)(2,1)S(1)} %slice.794), channel_id=1, source_target_pairs={{1,0},{2,1},{3,2},{4,3},{5,4},{6,5},{7,6},{9,8},{10,9},{11,10},{12... | collective-permute-start | bytes 968 | tf_op jit(solution)/shard_map/ppermute | solution.py:13
  13.2 8.8 %collective-permute-start.2 = (f32[2,20,1,128]{3,2,1,0:T(1,128)S(1)}, f32[2,20,1,128]{3,2,1,0:T(1,128)S(1)}, u32[]{:S(2)}, u32[]{:S(2)}) collective-permute-start(f32[2,20,1,128]{3,2,1,0:T(1,128)S(1)} %get-tuple-element.67), channel_id=1, source_target_pairs={{0,8},{8,16},{16,24},{24,32},{32,40},{40,48},{48,56},{56,64},{64,7... | collective-permute-start | bytes 61448 | tf_op jit(solution)/shard_map/ppermute | solution.py:24
  15.2 7.4 %collective-permute-start.3 = (f32[2,20,1,128]{3,2,1,0:T(1,128)S(1)}, f32[2,20,1,128]{3,2,1,0:T(1,128)S(1)}, u32[]{:S(2)}, u32[]{:S(2)}) collective-permute-start(f32[2,20,1,128]{3,2,1,0:T(1,128)S(1)} %get-tuple-element.68), channel_id=1, source_target_pairs={{8,0},{16,8},{24,16},{32,24},{40,32},{48,40},{56,48},{64,56},{72,6... | collective-permute-start | bytes 61448 | tf_op jit(solution)/shard_map/ppermute | solution.py:26
  22.7 12.1 %collective-permute-start.4 = (f32[2,20,10,1]{3,2,1,0:T(8,128)S(1)}, f32[2,20,10,1]{3,2,1,0:T(8,128)S(1)}, u32[]{:S(2)}, u32[]{:S(2)}) collective-permute-start(f32[2,20,10,1]{3,2,1,0:T(8,128)S(1)} %get-tuple-element.43), channel_id=1, source_target_pairs={{0,1},{1,2},{2,3},{3,4},{4,5},{5,6},{6,7},{8,9},{9,10},{10,11},{11... | collective-permute-start | bytes 4808 | tf_op jit(solution)/shard_map/ppermute | solution.py:24
  28.6 15.6 %collective-permute-start.5 = (f32[2,20,10,1]{3,2,1,0:T(8,128)S(1)}, f32[2,20,10,1]{3,2,1,0:T(8,128)S(1)}, u32[]{:S(2)}, u32[]{:S(2)}) collective-permute-start(f32[2,20,10,1]{3,2,1,0:T(8,128)S(1)} %get-tuple-element.44), channel_id=1, source_target_pairs={{1,0},{2,1},{3,2},{4,3},{5,4},{6,5},{7,6},{9,8},{10,9},{11,10},{12... | collective-permute-start | bytes 4808 | tf_op jit(solution)/shard_map/ppermute | solution.py:26
  45.6 7.7 %collective-permute-start.6 = (f32[2,20,1,128]{3,2,1,0:T(1,128)S(1)}, f32[2,20,1,128]{3,2,1,0:T(1,128)S(1)}, u32[]{:S(2)}, u32[]{:S(2)}) collective-permute-start(f32[2,20,1,128]{3,2,1,0:T(1,128)S(1)} %get-tuple-element.63), channel_id=1, source_target_pairs={{0,8},{8,16},{16,24},{24,32},{32,40},{40,48},{48,56},{56,64},{64,7... | collective-permute-start | bytes 61448 | tf_op jit(solution)/shard_map/ppermute | solution.py:24
  47.5 7.2 %collective-permute-start.7 = (f32[2,20,1,128]{3,2,1,0:T(1,128)S(1)}, f32[2,20,1,128]{3,2,1,0:T(1,128)S(1)}, u32[]{:S(2)}, u32[]{:S(2)}) collective-permute-start(f32[2,20,1,128]{3,2,1,0:T(1,128)S(1)} %get-tuple-element.64), channel_id=1, source_target_pairs={{8,0},{16,8},{24,16},{32,24},{40,32},{48,40},{56,48},{64,56},{72,6... | collective-permute-start | bytes 61448 | tf_op jit(solution)/shard_map/ppermute | solution.py:26
  54.9 9.2 %collective-permute-start.8 = (f32[2,20,10,1]{3,2,1,0:T(8,128)S(1)}, f32[2,20,10,1]{3,2,1,0:T(8,128)S(1)}, u32[]{:S(2)}, u32[]{:S(2)}) collective-permute-start(f32[2,20,10,1]{3,2,1,0:T(8,128)S(1)} %get-tuple-element.41), channel_id=1, source_target_pairs={{0,1},{1,2},{2,3},{3,4},{4,5},{5,6},{6,7},{8,9},{9,10},{10,11},{11... | collective-permute-start | bytes 4808 | tf_op jit(solution)/shard_map/ppermute | solution.py:24
  59.6 13.8 %collective-permute-start.9 = (f32[2,20,10,1]{3,2,1,0:T(8,128)S(1)}, f32[2,20,10,1]{3,2,1,0:T(8,128)S(1)}, u32[]{:S(2)}, u32[]{:S(2)}) collective-permute-start(f32[2,20,10,1]{3,2,1,0:T(8,128)S(1)} %get-tuple-element.42), channel_id=1, source_target_pairs={{1,0},{2,1},{3,2},{4,3},{5,4},{6,5},{7,6},{9,8},{10,9},{11,10},{12... | collective-permute-start | bytes 4808 | tf_op jit(solution)/shard_map/ppermute | solution.py:26
  73.8 7.7 %collective-permute-start.10 = (f32[2,20,1,128]{3,2,1,0:T(1,128)S(1)}, f32[2,20,1,128]{3,2,1,0:T(1,128)S(1)}, u32[]{:S(2)}, u32[]{:S(2)}) collective-permute-start(f32[2,20,1,128]{3,2,1,0:T(1,128)S(1)} %get-tuple-element.59), channel_id=1, source_target_pairs={{0,8},{8,16},{16,24},{24,32},{32,40},{40,48},{48,56},{56,64},{64,7... | collective-permute-start | bytes 61448 | tf_op jit(solution)/shard_map/ppermute | solution.py:24
  75.8 7.2 %collective-permute-start.11 = (f32[2,20,1,128]{3,2,1,0:T(1,128)S(1)}, f32[2,20,1,128]{3,2,1,0:T(1,128)S(1)}, u32[]{:S(2)}, u32[]{:S(2)}) collective-permute-start(f32[2,20,1,128]{3,2,1,0:T(1,128)S(1)} %get-tuple-element.60), channel_id=1, source_target_pairs={{8,0},{16,8},{24,16},{32,24},{40,32},{48,40},{56,48},{64,56},{72,6... | collective-permute-start | bytes 61448 | tf_op jit(solution)/shard_map/ppermute | solution.py:26
  83.2 10.2 %collective-permute-start.12 = (f32[2,20,10,1]{3,2,1,0:T(8,128)S(1)}, f32[2,20,10,1]{3,2,1,0:T(8,128)S(1)}, u32[]{:S(2)}, u32[]{:S(2)}) collective-permute-start(f32[2,20,10,1]{3,2,1,0:T(8,128)S(1)} %get-tuple-element.39), channel_id=1, source_target_pairs={{0,1},{1,2},{2,3},{3,4},{4,5},{5,6},{6,7},{8,9},{9,10},{10,11},{11... | collective-permute-start | bytes 4808 | tf_op jit(solution)/shard_map/ppermute | solution.py:24
  87.7 15.0 %collective-permute-start.13 = (f32[2,20,10,1]{3,2,1,0:T(8,128)S(1)}, f32[2,20,10,1]{3,2,1,0:T(8,128)S(1)}, u32[]{:S(2)}, u32[]{:S(2)}) collective-permute-start(f32[2,20,10,1]{3,2,1,0:T(8,128)S(1)} %get-tuple-element.40), channel_id=1, source_target_pairs={{1,0},{2,1},{3,2},{4,3},{5,4},{6,5},{7,6},{9,8},{10,9},{11,10},{12... | collective-permute-start | bytes 4808 | tf_op jit(solution)/shard_map/ppermute | solution.py:26
  103.4 7.8 %collective-permute-start.14 = (f32[2,20,1,128]{3,2,1,0:T(1,128)S(1)}, f32[2,20,1,128]{3,2,1,0:T(1,128)S(1)}, u32[]{:S(2)}, u32[]{:S(2)}) collective-permute-start(f32[2,20,1,128]{3,2,1,0:T(1,128)S(1)} %get-tuple-element.57), channel_id=1, source_target_pairs={{0,8},{8,16},{16,24},{24,32},{32,40},{40,48},{48,56},{56,64},{64,7... | collective-permute-start | bytes 61448 | tf_op jit(solution)/shard_map/ppermute | solution.py:24
  105.3 7.2 %collective-permute-start.15 = (f32[2,20,1,128]{3,2,1,0:T(1,128)S(1)}, f32[2,20,1,128]{3,2,1,0:T(1,128)S(1)}, u32[]{:S(2)}, u32[]{:S(2)}) collective-permute-start(f32[2,20,1,128]{3,2,1,0:T(1,128)S(1)} %get-tuple-element.58), channel_id=1, source_target_pairs={{8,0},{16,8},{24,16},{32,24},{40,32},{48,40},{56,48},{64,56},{72,6... | collective-permute-start | bytes 61448 | tf_op jit(solution)/shard_map/ppermute | solution.py:26
  112.7 9.1 %collective-permute-start.16 = (f32[2,20,10,1]{3,2,1,0:T(8,128)S(1)}, f32[2,20,10,1]{3,2,1,0:T(8,128)S(1)}, u32[]{:S(2)}, u32[]{:S(2)}) collective-permute-start(f32[2,20,10,1]{3,2,1,0:T(8,128)S(1)} %get-tuple-element.37), channel_id=1, source_target_pairs={{0,1},{1,2},{2,3},{3,4},{4,5},{5,6},{6,7},{8,9},{9,10},{10,11},{11... | collective-permute-start | bytes 4808 | tf_op jit(solution)/shard_map/ppermute | solution.py:24
  116.6 13.0 %collective-permute-start.17 = (f32[2,20,10,1]{3,2,1,0:T(8,128)S(1)}, f32[2,20,10,1]{3,2,1,0:T(8,128)S(1)}, u32[]{:S(2)}, u32[]{:S(2)}) collective-permute-start(f32[2,20,10,1]{3,2,1,0:T(8,128)S(1)} %get-tuple-element.38), channel_id=1, source_target_pairs={{1,0},{2,1},{3,2},{4,3},{5,4},{6,5},{7,6},{9,8},{10,9},{11,10},{12... | collective-permute-start | bytes 4808 | tf_op jit(solution)/shard_map/ppermute | solution.py:26
  130.1 7.7 %collective-permute-start.18 = (f32[2,20,1,128]{3,2,1,0:T(1,128)S(1)}, f32[2,20,1,128]{3,2,1,0:T(1,128)S(1)}, u32[]{:S(2)}, u32[]{:S(2)}) collective-permute-start(f32[2,20,1,128]{3,2,1,0:T(1,128)S(1)} %get-tuple-element.53), channel_id=1, source_target_pairs={{0,8},{8,16},{16,24},{24,32},{32,40},{40,48},{48,56},{56,64},{64,7... | collective-permute-start | bytes 61448 | tf_op jit(solution)/shard_map/ppermute | solution.py:24
  132.0 7.2 %collective-permute-start.19 = (f32[2,20,1,128]{3,2,1,0:T(1,128)S(1)}, f32[2,20,1,128]{3,2,1,0:T(1,128)S(1)}, u32[]{:S(2)}, u32[]{:S(2)}) collective-permute-start(f32[2,20,1,128]{3,2,1,0:T(1,128)S(1)} %get-tuple-element.54), channel_id=1, source_target_pairs={{8,0},{16,8},{24,16},{32,24},{40,32},{48,40},{56,48},{64,56},{72,6... | collective-permute-start | bytes 61448 | tf_op jit(solution)/shard_map/ppermute | solution.py:26
  139.5 7.7 %collective-permute-start.20 = (f32[2,20,10,1]{3,2,1,0:T(8,128)S(1)}, f32[2,20,10,1]{3,2,1,0:T(8,128)S(1)}, u32[]{:S(2)}, u32[]{:S(2)}) collective-permute-start(f32[2,20,10,1]{3,2,1,0:T(8,128)S(1)} %get-tuple-element.35), channel_id=1, source_target_pairs={{0,1},{1,2},{2,3},{3,4},{4,5},{5,6},{6,7},{8,9},{9,10},{10,11},{11... | collective-permute-start | bytes 4808 | tf_op jit(solution)/shard_map/ppermute | solution.py:24
  141.4 13.6 %collective-permute-start.21 = (f32[2,20,10,1]{3,2,1,0:T(8,128)S(1)}, f32[2,20,10,1]{3,2,1,0:T(8,128)S(1)}, u32[]{:S(2)}, u32[]{:S(2)}) collective-permute-start(f32[2,20,10,1]{3,2,1,0:T(8,128)S(1)} %get-tuple-element.36), channel_id=1, source_target_pairs={{1,0},{2,1},{3,2},{4,3},{5,4},{6,5},{7,6},{9,8},{10,9},{11,10},{12... | collective-permute-start | bytes 4808 | tf_op jit(solution)/shard_map/ppermute | solution.py:26
  155.4 9.6 %collective-permute-start.22 = (f32[2,20,1,128]{3,2,1,0:T(1,128)S(1)}, f32[2,20,1,128]{3,2,1,0:T(1,128)S(1)}, u32[]{:S(2)}, u32[]{:S(2)}) collective-permute-start(f32[2,20,1,128]{3,2,1,0:T(1,128)S(1)} %get-tuple-element.49), channel_id=1, source_target_pairs={{0,8},{8,16},{16,24},{24,32},{32,40},{40,48},{48,56},{56,64},{64,7... | collective-permute-start | bytes 61448 | tf_op jit(solution)/shard_map/ppermute | solution.py:24
  157.3 7.7 %collective-permute-start.23 = (f32[2,20,1,128]{3,2,1,0:T(1,128)S(1)}, f32[2,20,1,128]{3,2,1,0:T(1,128)S(1)}, u32[]{:S(2)}, u32[]{:S(2)}) collective-permute-start(f32[2,20,1,128]{3,2,1,0:T(1,128)S(1)} %get-tuple-element.50), channel_id=1, source_target_pairs={{8,0},{16,8},{24,16},{32,24},{40,32},{48,40},{56,48},{64,56},{72,6... | collective-permute-start | bytes 61448 | tf_op jit(solution)/shard_map/ppermute | solution.py:26
  166.8 13.0 %collective-permute-start.25 = (f32[2,20,10,1]{3,2,1,0:T(8,128)S(1)}, f32[2,20,10,1]{3,2,1,0:T(8,128)S(1)}, u32[]{:S(2)}, u32[]{:S(2)}) collective-permute-start(f32[2,20,10,1]{3,2,1,0:T(8,128)S(1)} %get-tuple-element.34), channel_id=1, source_target_pairs={{1,0},{2,1},{3,2},{4,3},{5,4},{6,5},{7,6},{9,8},{10,9},{11,10},{12... | collective-permute-start | bytes 4808 | tf_op jit(solution)/shard_map/ppermute | solution.py:26
  (9 other events, 548.1 us)
where the time goes:
time: 322 us; the launch traced here: 321 us
  blocking collectives  129 us (40%)
  waiting for transfers between devices  85.2 us (26%)
  starting transfers between devices  79.7 us (25%)
  local copies, waits for them, and re-layouts  12.6 us (4%)
  other arithmetic  11.9 us (4%)
    unnamed x1, blocking collectives  108 us
    ppermute x12, waiting for transfers between devices, extended(): lax.ppermute(head, axis, [((i + 1) % count, i) for i in range(ends)])  57.5 us
    ppermute x12, starting transfers between devices, extended(): lax.ppermute(head, axis, [((i + 1) % count, i) for i in range(ends)])  42.4 us
    ppermute x12, starting transfers between devices, extended(): lax.ppermute(tail, axis, [(i, (i + 1) % count) for i in range(ends)])  33.6 us
    ppermute x12, waiting for transfers between devices, extended(): lax.ppermute(tail, axis, [(i, (i + 1) % count) for i in range(ends)])  24.9 us
    psum x1, blocking collectives, per_device(): well_partials = lax.psum(owned, 'gy')  20.5 us
  transfers between devices with their start and end apart: 26, of which 18 were waited for; matrix products, arithmetic and copies ran while one was open for 1% of the time, Pallas kernels for 0%

commit v1 on v0

--- a/solution.py
+++ b/solution.py
@@ -138,7 +138,7 @@
         picked, onehot, precision=lax.Precision.HIGHEST, preferred_element_type=jnp.float32
     )
     owned = lax.psum_scatter(partial_value, "gx", scatter_dimension=1, tiled=True)
-    well_partials = lax.psum(owned, "gy")
+    well_partials = jnp.sum(lax.all_gather(owned, "gy"), axis=0)
     return (adjoint_early, well_partials)
 
 

time: 322 us -> 332 us (1.031)
  blocking collectives: 129 us -> 139 us
    all_gather x0 -> x1, blocking collectives: none -> 30.6 us  [per_device(): well_partials = jnp.sum(lax.all_gather(owned, 'gy'), axis=0)]
    psum x1 -> x0, blocking collectives: 20.5 us -> none  [per_device(): well_partials = lax.psum(owned, 'gy')]
where the time goes in v1:
time: 332 us; the launch traced here: 331 us
  blocking collectives  139 us (42%)
  waiting for transfers between devices  85.2 us (26%)
  starting transfers between devices  79.7 us (24%)
  local copies, waits for them, and re-layouts  12.6 us (4%)
  other arithmetic  12.5 us (4%)
    unnamed x1, blocking collectives  108 us
    ppermute x12, waiting for transfers between devices, extended(): lax.ppermute(head, axis, [((i + 1) % count, i) for i in range(ends)])  57.5 us
    ppermute x12, starting transfers between devices, extended(): lax.ppermute(head, axis, [((i + 1) % count, i) for i in range(ends)])  42.4 us
    ppermute x12, starting transfers between devices, extended(): lax.ppermute(tail, axis, [(i, (i + 1) % count) for i in range(ends)])  33.6 us
    all_gather x1, blocking collectives, per_device(): well_partials = jnp.sum(lax.all_gather(owned, 'gy'), axis=0)  30.6 us
    ppermute x12, waiting for transfers between devices, extended(): lax.ppermute(tail, axis, [(i, (i + 1) % count) for i in range(ends)])  24.9 us
  transfers between devices with their start and end apart: 26, of which 18 were waited for; matrix products, arithmetic and copies ran while one was open for 1% of the time, Pallas kernels for 0%

profile of v1, /device:TPU:128, one launch (start us, length us, event | category | flops | bytes accessed | tf_op | source)
XLA Modules:
  0.0 331.2 jit_solution(18151090187962651070)
XLA Ops:
  15.2 5.9 %collective-permute-start.3 = (f32[2,20,1,128]{3,2,1,0:T(1,128)S(1)}, f32[2,20,1,128]{3,2,1,0:T(1,128)S(1)}, u32[]{:S(2)}, u32[]{:S(2)}) collective-permute-start(f32[2,20,1,128]{3,2,1,0:T(1,128)S(1)} %get-tuple-element.68), channel_id=1, source_target_pairs={{8,0},{16,8},{24,16},{32,24},{40,32},{48,40},{56,48},{64,56},{72,6... | collective-permute-start | bytes 61448 | tf_op jit(solution)/shard_map/ppermute | solution.py:26
  22.7 5.8 %collective-permute-start.4 = (f32[2,20,10,1]{3,2,1,0:T(8,128)S(1)}, f32[2,20,10,1]{3,2,1,0:T(8,128)S(1)}, u32[]{:S(2)}, u32[]{:S(2)}) collective-permute-start(f32[2,20,10,1]{3,2,1,0:T(8,128)S(1)} %get-tuple-element.43), channel_id=1, source_target_pairs={{0,1},{1,2},{2,3},{3,4},{4,5},{5,6},{6,7},{8,9},{9,10},{10,11},{11... | collective-permute-start | bytes 4808 | tf_op jit(solution)/shard_map/ppermute | solution.py:24
  29.9 5.0 %collective-permute-done.4 = f32[2,20,10,1]{3,2,1,0:T(8,128)S(1)} collective-permute-done((f32[2,20,10,1]{3,2,1,0:T(8,128)S(1)}, f32[2,20,10,1]{3,2,1,0:T(8,128)S(1)}, u32[]{:S(2)}, u32[]{:S(2)}) %collective-permute-start.4) | collective-permute-done | bytes 1632 | tf_op jit(solution)/shard_map/ppermute | solution.py:24
  34.9 9.3 %collective-permute-done.5 = f32[2,20,10,1]{3,2,1,0:T(8,128)S(1)} collective-permute-done((f32[2,20,10,1]{3,2,1,0:T(8,128)S(1)}, f32[2,20,10,1]{3,2,1,0:T(8,128)S(1)}, u32[]{:S(2)}, u32[]{:S(2)}) %collective-permute-start.5) | collective-permute-done | bytes 1632 | tf_op jit(solution)/shard_map/ppermute | solution.py:26
  47.5 5.8 %collective-permute-start.7 = (f32[2,20,1,128]{3,2,1,0:T(1,128)S(1)}, f32[2,20,1,128]{3,2,1,0:T(1,128)S(1)}, u32[]{:S(2)}, u32[]{:S(2)}) collective-permute-start(f32[2,20,1,128]{3,2,1,0:T(1,128)S(1)} %get-tuple-element.64), channel_id=1, source_target_pairs={{8,0},{16,8},{24,16},{32,24},{40,32},{48,40},{56,48},{64,56},{72,6... | collective-permute-start | bytes 61448 | tf_op jit(solution)/shard_map/ppermute | solution.py:26
  54.9 4.6 %collective-permute-start.8 = (f32[2,20,10,1]{3,2,1,0:T(8,128)S(1)}, f32[2,20,10,1]{3,2,1,0:T(8,128)S(1)}, u32[]{:S(2)}, u32[]{:S(2)}) collective-permute-start(f32[2,20,10,1]{3,2,1,0:T(8,128)S(1)} %get-tuple-element.41), channel_id=1, source_target_pairs={{0,1},{1,2},{2,3},{3,4},{4,5},{5,6},{6,7},{8,9},{9,10},{10,11},{11... | collective-permute-start | bytes 4808 | tf_op jit(solution)/shard_map/ppermute | solution.py:24
  64.1 9.3 %collective-permute-done.9 = f32[2,20,10,1]{3,2,1,0:T(8,128)S(1)} collective-permute-done((f32[2,20,10,1]{3,2,1,0:T(8,128)S(1)}, f32[2,20,10,1]{3,2,1,0:T(8,128)S(1)}, u32[]{:S(2)}, u32[]{:S(2)}) %collective-permute-start.9) | collective-permute-done | bytes 1632 | tf_op jit(solution)/shard_map/ppermute | solution.py:26
  75.8 5.8 %collective-permute-start.11 = (f32[2,20,1,128]{3,2,1,0:T(1,128)S(1)}, f32[2,20,1,128]{3,2,1,0:T(1,128)S(1)}, u32[]{:S(2)}, u32[]{:S(2)}) collective-permute-start(f32[2,20,1,128]{3,2,1,0:T(1,128)S(1)} %get-tuple-element.60), channel_id=1, source_target_pairs={{8,0},{16,8},{24,16},{32,24},{40,32},{48,40},{56,48},{64,56},{72,6... | collective-permute-start | bytes 61448 | tf_op jit(solution)/shard_map/ppermute | solution.py:26
  83.2 4.5 %collective-permute-start.12 = (f32[2,20,10,1]{3,2,1,0:T(8,128)S(1)}, f32[2,20,10,1]{3,2,1,0:T(8,128)S(1)}, u32[]{:S(2)}, u32[]{:S(2)}) collective-permute-start(f32[2,20,10,1]{3,2,1,0:T(8,128)S(1)} %get-tuple-element.39), channel_id=1, source_target_pairs={{0,1},{1,2},{2,3},{3,4},{4,5},{5,6},{6,7},{8,9},{9,10},{10,11},{11... | collective-permute-start | bytes 4808 | tf_op jit(solution)/shard_map/ppermute | solution.py:24
  89.0 4.4 %collective-permute-done.12 = f32[2,20,10,1]{3,2,1,0:T(8,128)S(1)} collective-permute-done((f32[2,20,10,1]{3,2,1,0:T(8,128)S(1)}, f32[2,20,10,1]{3,2,1,0:T(8,128)S(1)}, u32[]{:S(2)}, u32[]{:S(2)}) %collective-permute-start.12) | collective-permute-done | bytes 1632 | tf_op jit(solution)/shard_map/ppermute | solution.py:24
  93.4 9.3 %collective-permute-done.13 = f32[2,20,10,1]{3,2,1,0:T(8,128)S(1)} collective-permute-done((f32[2,20,10,1]{3,2,1,0:T(8,128)S(1)}, f32[2,20,10,1]{3,2,1,0:T(8,128)S(1)}, u32[]{:S(2)}, u32[]{:S(2)}) %collective-permute-start.13) | collective-permute-done | bytes 1632 | tf_op jit(solution)/shard_map/ppermute | solution.py:26
  105.3 5.8 %collective-permute-start.15 = (f32[2,20,1,128]{3,2,1,0:T(1,128)S(1)}, f32[2,20,1,128]{3,2,1,0:T(1,128)S(1)}, u32[]{:S(2)}, u32[]{:S(2)}) collective-permute-start(f32[2,20,1,128]{3,2,1,0:T(1,128)S(1)} %get-tuple-element.58), channel_id=1, source_target_pairs={{8,0},{16,8},{24,16},{32,24},{40,32},{48,40},{56,48},{64,56},{72,6... | collective-permute-start | bytes 61448 | tf_op jit(solution)/shard_map/ppermute | solution.py:26
  117.9 4.0 %collective-permute-done.16 = f32[2,20,10,1]{3,2,1,0:T(8,128)S(1)} collective-permute-done((f32[2,20,10,1]{3,2,1,0:T(8,128)S(1)}, f32[2,20,10,1]{3,2,1,0:T(8,128)S(1)}, u32[]{:S(2)}, u32[]{:S(2)}) %collective-permute-start.16) | collective-permute-done | bytes 1632 | tf_op jit(solution)/shard_map/ppermute | solution.py:24
  121.9 7.8 %collective-permute-done.17 = f32[2,20,10,1]{3,2,1,0:T(8,128)S(1)} collective-permute-done((f32[2,20,10,1]{3,2,1,0:T(8,128)S(1)}, f32[2,20,10,1]{3,2,1,0:T(8,128)S(1)}, u32[]{:S(2)}, u32[]{:S(2)}) %collective-permute-start.17) | collective-permute-done | bytes 1632 | tf_op jit(solution)/shard_map/ppermute | solution.py:26
  132.0 5.8 %collective-permute-start.19 = (f32[2,20,1,128]{3,2,1,0:T(1,128)S(1)}, f32[2,20,1,128]{3,2,1,0:T(1,128)S(1)}, u32[]{:S(2)}, u32[]{:S(2)}) collective-permute-start(f32[2,20,1,128]{3,2,1,0:T(1,128)S(1)} %get-tuple-element.54), channel_id=1, source_target_pairs={{8,0},{16,8},{24,16},{32,24},{40,32},{48,40},{56,48},{64,56},{72,6... | collective-permute-start | bytes 61448 | tf_op jit(solution)/shard_map/ppermute | solution.py:26
  142.7 4.5 %collective-permute-done.20 = f32[2,20,10,1]{3,2,1,0:T(8,128)S(1)} collective-permute-done((f32[2,20,10,1]{3,2,1,0:T(8,128)S(1)}, f32[2,20,10,1]{3,2,1,0:T(8,128)S(1)}, u32[]{:S(2)}, u32[]{:S(2)}) %collective-permute-start.20) | collective-permute-done | bytes 1632 | tf_op jit(solution)/shard_map/ppermute | solution.py:24
  147.2 7.8 %collective-permute-done.21 = f32[2,20,10,1]{3,2,1,0:T(8,128)S(1)} collective-permute-done((f32[2,20,10,1]{3,2,1,0:T(8,128)S(1)}, f32[2,20,10,1]{3,2,1,0:T(8,128)S(1)}, u32[]{:S(2)}, u32[]{:S(2)}) %collective-permute-start.21) | collective-permute-done | bytes 1632 | tf_op jit(solution)/shard_map/ppermute | solution.py:26
  157.3 5.8 %collective-permute-start.23 = (f32[2,20,1,128]{3,2,1,0:T(1,128)S(1)}, f32[2,20,1,128]{3,2,1,0:T(1,128)S(1)}, u32[]{:S(2)}, u32[]{:S(2)}) collective-permute-start(f32[2,20,1,128]{3,2,1,0:T(1,128)S(1)} %get-tuple-element.50), channel_id=1, source_target_pairs={{8,0},{16,8},{24,16},{32,24},{40,32},{48,40},{56,48},{64,56},{72,6... | collective-permute-start | bytes 61448 | tf_op jit(solution)/shard_map/ppermute | solution.py:26
  168.1 3.9 %collective-permute-done.24 = f32[2,20,10,1]{3,2,1,0:T(8,128)S(1)} collective-permute-done((f32[2,20,10,1]{3,2,1,0:T(8,128)S(1)}, f32[2,20,10,1]{3,2,1,0:T(8,128)S(1)}, u32[]{:S(2)}, u32[]{:S(2)}) %collective-permute-start.24) | collective-permute-done | bytes 1632 | tf_op jit(solution)/shard_map/ppermute | solution.py:24
  172.0 7.8 %collective-permute-done.25 = f32[2,20,10,1]{3,2,1,0:T(8,128)S(1)} collective-permute-done((f32[2,20,10,1]{3,2,1,0:T(8,128)S(1)}, f32[2,20,10,1]{3,2,1,0:T(8,128)S(1)}, u32[]{:S(2)}, u32[]{:S(2)}) %collective-permute-start.25) | collective-permute-done | bytes 1632 | tf_op jit(solution)/shard_map/ppermute | solution.py:26
  181.1 5.5 %copy.17 = f32[4,20480]{0,1:T(8,128)} copy(f32[4,20480]{1,0:T(4,128)S(1)} %pad_maximum_fusion.6) | data formatting | bytes 655360 | tf_op jit(solution)/shard_map/concatenate | solution.py:131
  186.7 4.7 %gather_fusion = f32[256,4]{1,0:T(8,128)S(1)} fusion(f32[4,20480]{0,1:T(8,128)} %copy.17, s32[1024]{0:T(1024)S(1)} %pad_clamp_fusion), kind=kCustom, calls=%fused_computation | custom fusion | bytes 9216 | tf_op jit(solution)/shard_map/jit(_take)/gather | solution.py:134
  191.8 108.2 %all-reduce.13 = f32[4,512]{1,0:T(4,128)S(1)} all-reduce(f32[4,512]{1,0:T(4,128)S(1)} %fusion), channel_id=3, replica_groups=mesh['gx'=64,'gy'=8] {'gx'}, use_global_device_ids=true, to_apply=%region_0.1.clone | all-reduce | flops 2048 | bytes 16384
  300.0 30.6 %all-gather.1 = f32[8,4,8]{2,1,0:T(4,128)S(1)} all-gather(f32[1,4,8]{2,1,0:T(4,128)S(1)} %dynamic-slice_bitcast_fusion), channel_id=2, replica_groups=mesh['gx'=64,'gy'=8] {'gy'}, dimensions={0}, use_global_device_ids=true | all-gather | bytes 1152 | tf_op jit(solution)/shard_map/all_gather | solution.py:141
  (124 shorter events, 57.6 us)
Async XLA Ops:
  1.6 7.4 %collective-permute-start.1 = (bf16[20,8,1]{2,1,0:T(8,128)(2,1)S(1)}, bf16[20,8,1]{2,1,0:T(8,128)(2,1)S(1)}, u32[]{:S(2)}, u32[]{:S(2)}) collective-permute-start(bf16[20,8,1]{2,1,0:T(8,128)(2,1)S(1)} %slice.794), channel_id=1, source_target_pairs={{1,0},{2,1},{3,2},{4,3},{5,4},{6,5},{7,6},{9,8},{10,9},{11,10},{12... | collective-permute-start | bytes 968 | tf_op jit(solution)/shard_map/ppermute | solution.py:13
  13.2 8.8 %collective-permute-start.2 = (f32[2,20,1,128]{3,2,1,0:T(1,128)S(1)}, f32[2,20,1,128]{3,2,1,0:T(1,128)S(1)}, u32[]{:S(2)}, u32[]{:S(2)}) collective-permute-start(f32[2,20,1,128]{3,2,1,0:T(1,128)S(1)} %get-tuple-element.67), channel_id=1, source_target_pairs={{0,8},{8,16},{16,24},{24,32},{32,40},{40,48},{48,56},{56,64},{64,7... | collective-permute-start | bytes 61448 | tf_op jit(solution)/shard_map/ppermute | solution.py:24
  15.2 7.4 %collective-permute-start.3 = (f32[2,20,1,128]{3,2,1,0:T(1,128)S(1)}, f32[2,20,1,128]{3,2,1,0:T(1,128)S(1)}, u32[]{:S(2)}, u32[]{:S(2)}) collective-permute-start(f32[2,20,1,128]{3,2,1,0:T(1,128)S(1)} %get-tuple-element.68), channel_id=1, source_target_pairs={{8,0},{16,8},{24,16},{32,24},{40,32},{48,40},{56,48},{64,56},{72,6... | collective-permute-start | bytes 61448 | tf_op jit(solution)/shard_map/ppermute | solution.py:26
  22.7 12.1 %collective-permute-start.4 = (f32[2,20,10,1]{3,2,1,0:T(8,128)S(1)}, f32[2,20,10,1]{3,2,1,0:T(8,128)S(1)}, u32[]{:S(2)}, u32[]{:S(2)}) collective-permute-start(f32[2,20,10,1]{3,2,1,0:T(8,128)S(1)} %get-tuple-element.43), channel_id=1, source_target_pairs={{0,1},{1,2},{2,3},{3,4},{4,5},{5,6},{6,7},{8,9},{9,10},{10,11},{11... | collective-permute-start | bytes 4808 | tf_op jit(solution)/shard_map/ppermute | solution.py:24
  28.6 15.6 %collective-permute-start.5 = (f32[2,20,10,1]{3,2,1,0:T(8,128)S(1)}, f32[2,20,10,1]{3,2,1,0:T(8,128)S(1)}, u32[]{:S(2)}, u32[]{:S(2)}) collective-permute-start(f32[2,20,10,1]{3,2,1,0:T(8,128)S(1)} %get-tuple-element.44), channel_id=1, source_target_pairs={{1,0},{2,1},{3,2},{4,3},{5,4},{6,5},{7,6},{9,8},{10,9},{11,10},{12... | collective-permute-start | bytes 4808 | tf_op jit(solution)/shard_map/ppermute | solution.py:26
  45.6 7.7 %collective-permute-start.6 = (f32[2,20,1,128]{3,2,1,0:T(1,128)S(1)}, f32[2,20,1,128]{3,2,1,0:T(1,128)S(1)}, u32[]{:S(2)}, u32[]{:S(2)}) collective-permute-start(f32[2,20,1,128]{3,2,1,0:T(1,128)S(1)} %get-tuple-element.63), channel_id=1, source_target_pairs={{0,8},{8,16},{16,24},{24,32},{32,40},{40,48},{48,56},{56,64},{64,7... | collective-permute-start | bytes 61448 | tf_op jit(solution)/shard_map/ppermute | solution.py:24
  47.5 7.2 %collective-permute-start.7 = (f32[2,20,1,128]{3,2,1,0:T(1,128)S(1)}, f32[2,20,1,128]{3,2,1,0:T(1,128)S(1)}, u32[]{:S(2)}, u32[]{:S(2)}) collective-permute-start(f32[2,20,1,128]{3,2,1,0:T(1,128)S(1)} %get-tuple-element.64), channel_id=1, source_target_pairs={{8,0},{16,8},{24,16},{32,24},{40,32},{48,40},{56,48},{64,56},{72,6... | collective-permute-start | bytes 61448 | tf_op jit(solution)/shard_map/ppermute | solution.py:26
  54.9 9.2 %collective-permute-start.8 = (f32[2,20,10,1]{3,2,1,0:T(8,128)S(1)}, f32[2,20,10,1]{3,2,1,0:T(8,128)S(1)}, u32[]{:S(2)}, u32[]{:S(2)}) collective-permute-start(f32[2,20,10,1]{3,2,1,0:T(8,128)S(1)} %get-tuple-element.41), channel_id=1, source_target_pairs={{0,1},{1,2},{2,3},{3,4},{4,5},{5,6},{6,7},{8,9},{9,10},{10,11},{11... | collective-permute-start | bytes 4808 | tf_op jit(solution)/shard_map/ppermute | solution.py:24
  59.6 13.8 %collective-permute-start.9 = (f32[2,20,10,1]{3,2,1,0:T(8,128)S(1)}, f32[2,20,10,1]{3,2,1,0:T(8,128)S(1)}, u32[]{:S(2)}, u32[]{:S(2)}) collective-permute-start(f32[2,20,10,1]{3,2,1,0:T(8,128)S(1)} %get-tuple-element.42), channel_id=1, source_target_pairs={{1,0},{2,1},{3,2},{4,3},{5,4},{6,5},{7,6},{9,8},{10,9},{11,10},{12... | collective-permute-start | bytes 4808 | tf_op jit(solution)/shard_map/ppermute | solution.py:26
  73.8 7.7 %collective-permute-start.10 = (f32[2,20,1,128]{3,2,1,0:T(1,128)S(1)}, f32[2,20,1,128]{3,2,1,0:T(1,128)S(1)}, u32[]{:S(2)}, u32[]{:S(2)}) collective-permute-start(f32[2,20,1,128]{3,2,1,0:T(1,128)S(1)} %get-tuple-element.59), channel_id=1, source_target_pairs={{0,8},{8,16},{16,24},{24,32},{32,40},{40,48},{48,56},{56,64},{64,7... | collective-permute-start | bytes 61448 | tf_op jit(solution)/shard_map/ppermute | solution.py:24
  75.8 7.2 %collective-permute-start.11 = (f32[2,20,1,128]{3,2,1,0:T(1,128)S(1)}, f32[2,20,1,128]{3,2,1,0:T(1,128)S(1)}, u32[]{:S(2)}, u32[]{:S(2)}) collective-permute-start(f32[2,20,1,128]{3,2,1,0:T(1,128)S(1)} %get-tuple-element.60), channel_id=1, source_target_pairs={{8,0},{16,8},{24,16},{32,24},{40,32},{48,40},{56,48},{64,56},{72,6... | collective-permute-start | bytes 61448 | tf_op jit(solution)/shard_map/ppermute | solution.py:26
  83.2 10.2 %collective-permute-start.12 = (f32[2,20,10,1]{3,2,1,0:T(8,128)S(1)}, f32[2,20,10,1]{3,2,1,0:T(8,128)S(1)}, u32[]{:S(2)}, u32[]{:S(2)}) collective-permute-start(f32[2,20,10,1]{3,2,1,0:T(8,128)S(1)} %get-tuple-element.39), channel_id=1, source_target_pairs={{0,1},{1,2},{2,3},{3,4},{4,5},{5,6},{6,7},{8,9},{9,10},{10,11},{11... | collective-permute-start | bytes 4808 | tf_op jit(solution)/shard_map/ppermute | solution.py:24
  87.7 15.0 %collective-permute-start.13 = (f32[2,20,10,1]{3,2,1,0:T(8,128)S(1)}, f32[2,20,10,1]{3,2,1,0:T(8,128)S(1)}, u32[]{:S(2)}, u32[]{:S(2)}) collective-permute-start(f32[2,20,10,1]{3,2,1,0:T(8,128)S(1)} %get-tuple-element.40), channel_id=1, source_target_pairs={{1,0},{2,1},{3,2},{4,3},{5,4},{6,5},{7,6},{9,8},{10,9},{11,10},{12... | collective-permute-start | bytes 4808 | tf_op jit(solution)/shard_map/ppermute | solution.py:26
  103.4 7.8 %collective-permute-start.14 = (f32[2,20,1,128]{3,2,1,0:T(1,128)S(1)}, f32[2,20,1,128]{3,2,1,0:T(1,128)S(1)}, u32[]{:S(2)}, u32[]{:S(2)}) collective-permute-start(f32[2,20,1,128]{3,2,1,0:T(1,128)S(1)} %get-tuple-element.57), channel_id=1, source_target_pairs={{0,8},{8,16},{16,24},{24,32},{32,40},{40,48},{48,56},{56,64},{64,7... | collective-permute-start | bytes 61448 | tf_op jit(solution)/shard_map/ppermute | solution.py:24
  105.3 7.2 %collective-permute-start.15 = (f32[2,20,1,128]{3,2,1,0:T(1,128)S(1)}, f32[2,20,1,128]{3,2,1,0:T(1,128)S(1)}, u32[]{:S(2)}, u32[]{:S(2)}) collective-permute-start(f32[2,20,1,128]{3,2,1,0:T(1,128)S(1)} %get-tuple-element.58), channel_id=1, source_target_pairs={{8,0},{16,8},{24,16},{32,24},{40,32},{48,40},{56,48},{64,56},{72,6... | collective-permute-start | bytes 61448 | tf_op jit(solution)/shard_map/ppermute | solution.py:26
  112.7 9.1 %collective-permute-start.16 = (f32[2,20,10,1]{3,2,1,0:T(8,128)S(1)}, f32[2,20,10,1]{3,2,1,0:T(8,128)S(1)}, u32[]{:S(2)}, u32[]{:S(2)}) collective-permute-start(f32[2,20,10,1]{3,2,1,0:T(8,128)S(1)} %get-tuple-element.37), channel_id=1, source_target_pairs={{0,1},{1,2},{2,3},{3,4},{4,5},{5,6},{6,7},{8,9},{9,10},{10,11},{11... | collective-permute-start | bytes 4808 | tf_op jit(solution)/shard_map/ppermute | solution.py:24
  116.6 13.0 %collective-permute-start.17 = (f32[2,20,10,1]{3,2,1,0:T(8,128)S(1)}, f32[2,20,10,1]{3,2,1,0:T(8,128)S(1)}, u32[]{:S(2)}, u32[]{:S(2)}) collective-permute-start(f32[2,20,10,1]{3,2,1,0:T(8,128)S(1)} %get-tuple-element.38), channel_id=1, source_target_pairs={{1,0},{2,1},{3,2},{4,3},{5,4},{6,5},{7,6},{9,8},{10,9},{11,10},{12... | collective-permute-start | bytes 4808 | tf_op jit(solution)/shard_map/ppermute | solution.py:26
  130.1 7.7 %collective-permute-start.18 = (f32[2,20,1,128]{3,2,1,0:T(1,128)S(1)}, f32[2,20,1,128]{3,2,1,0:T(1,128)S(1)}, u32[]{:S(2)}, u32[]{:S(2)}) collective-permute-start(f32[2,20,1,128]{3,2,1,0:T(1,128)S(1)} %get-tuple-element.53), channel_id=1, source_target_pairs={{0,8},{8,16},{16,24},{24,32},{32,40},{40,48},{48,56},{56,64},{64,7... | collective-permute-start | bytes 61448 | tf_op jit(solution)/shard_map/ppermute | solution.py:24
  132.0 7.2 %collective-permute-start.19 = (f32[2,20,1,128]{3,2,1,0:T(1,128)S(1)}, f32[2,20,1,128]{3,2,1,0:T(1,128)S(1)}, u32[]{:S(2)}, u32[]{:S(2)}) collective-permute-start(f32[2,20,1,128]{3,2,1,0:T(1,128)S(1)} %get-tuple-element.54), channel_id=1, source_target_pairs={{8,0},{16,8},{24,16},{32,24},{40,32},{48,40},{56,48},{64,56},{72,6... | collective-permute-start | bytes 61448 | tf_op jit(solution)/shard_map/ppermute | solution.py:26
  139.5 7.7 %collective-permute-start.20 = (f32[2,20,10,1]{3,2,1,0:T(8,128)S(1)}, f32[2,20,10,1]{3,2,1,0:T(8,128)S(1)}, u32[]{:S(2)}, u32[]{:S(2)}) collective-permute-start(f32[2,20,10,1]{3,2,1,0:T(8,128)S(1)} %get-tuple-element.35), channel_id=1, source_target_pairs={{0,1},{1,2},{2,3},{3,4},{4,5},{5,6},{6,7},{8,9},{9,10},{10,11},{11... | collective-permute-start | bytes 4808 | tf_op jit(solution)/shard_map/ppermute | solution.py:24
  141.4 13.6 %collective-permute-start.21 = (f32[2,20,10,1]{3,2,1,0:T(8,128)S(1)}, f32[2,20,10,1]{3,2,1,0:T(8,128)S(1)}, u32[]{:S(2)}, u32[]{:S(2)}) collective-permute-start(f32[2,20,10,1]{3,2,1,0:T(8,128)S(1)} %get-tuple-element.36), channel_id=1, source_target_pairs={{1,0},{2,1},{3,2},{4,3},{5,4},{6,5},{7,6},{9,8},{10,9},{11,10},{12... | collective-permute-start | bytes 4808 | tf_op jit(solution)/shard_map/ppermute | solution.py:26
  155.4 9.6 %collective-permute-start.22 = (f32[2,20,1,128]{3,2,1,0:T(1,128)S(1)}, f32[2,20,1,128]{3,2,1,0:T(1,128)S(1)}, u32[]{:S(2)}, u32[]{:S(2)}) collective-permute-start(f32[2,20,1,128]{3,2,1,0:T(1,128)S(1)} %get-tuple-element.49), channel_id=1, source_target_pairs={{0,8},{8,16},{16,24},{24,32},{32,40},{40,48},{48,56},{56,64},{64,7... | collective-permute-start | bytes 61448 | tf_op jit(solution)/shard_map/ppermute | solution.py:24
  157.3 7.7 %collective-permute-start.23 = (f32[2,20,1,128]{3,2,1,0:T(1,128)S(1)}, f32[2,20,1,128]{3,2,1,0:T(1,128)S(1)}, u32[]{:S(2)}, u32[]{:S(2)}) collective-permute-start(f32[2,20,1,128]{3,2,1,0:T(1,128)S(1)} %get-tuple-element.50), channel_id=1, source_target_pairs={{8,0},{16,8},{24,16},{32,24},{40,32},{48,40},{56,48},{64,56},{72,6... | collective-permute-start | bytes 61448 | tf_op jit(solution)/shard_map/ppermute | solution.py:26
  166.8 13.0 %collective-permute-start.25 = (f32[2,20,10,1]{3,2,1,0:T(8,128)S(1)}, f32[2,20,10,1]{3,2,1,0:T(8,128)S(1)}, u32[]{:S(2)}, u32[]{:S(2)}) collective-permute-start(f32[2,20,10,1]{3,2,1,0:T(8,128)S(1)} %get-tuple-element.34), channel_id=1, source_target_pairs={{1,0},{2,1},{3,2},{4,3},{5,4},{6,5},{7,6},{9,8},{10,9},{11,10},{12... | collective-permute-start | bytes 4808 | tf_op jit(solution)/shard_map/ppermute | solution.py:26
  (9 other events, 548.1 us)
